TPU v7x, 32 devices: a whole 2x2x4 slice. The times are simulated.
32 devices in a mesh: ccd: 8 (over z, x), tile: 4 (over y, core).
Axes of the slice: x: 2, y: 2, z: 4, core: 2. Of those that a mesh axis runs over, the one named last changes fastest.
Arguments:
- visit_image: bfloat16 [4096, 1024], P(('ccd', 'tile')), may hold values from -6 to 6
- mask_bits: int32 [4096, 1024], P(('ccd', 'tile')), may hold values from 0 to 15
- visit_weight: float32 [8], P('ccd'), may hold values from 1 to 4
- basis_cols: bfloat16 [31, 21], replicated, may hold values from -1.25 to 1.25
- basis_rows: bfloat16 [31, 21], replicated, may hold values from -1.25 to 1.25
- kernel_coef: float32 [8, 31, 6], P('ccd'), may hold values from -1 to 1
- row_warp: bfloat16 [4096, 512], P(('ccd', 'tile')), may hold values from -1 to 1, as said below
- col_warp: bfloat16 [8, 1024, 1024], P('ccd'), may hold values from -1 to 1, as said below
- dest_owner: int32 [2048, 1], P(('ccd', 'tile')), may hold values from 0 to 7; in each aligned block of 64 rows (0 to 63, 64 to 127, ...) at most 16 rows name the same one
- dest_block: int32 [2048], P(('ccd', 'tile')), may hold values from 0 to 63
- new_science: float32 [4096, 1024], P(('ccd', 'tile')), may hold values from -6 to 6
- tmpl_owner: int32 [2048, 1], P(('ccd', 'tile')), may hold values from 0 to 7; in each aligned block of 64 rows (0 to 63, 64 to 127, ...) at most 16 rows name the same one
- tmpl_block: int32 [2048], P(('ccd', 'tile')), may hold values from 0 to 63
Outputs:
- coadd: float32 [4096, 1024], P(('ccd', 'tile'))
- difference: float32 [4096, 1024], P(('ccd', 'tile'))
Inputs may be any that keep to these rules, and one draw needn't show every extreme that they name: `dest_owner`: within the 64 rows of one device no patch is named more than 16 times, a bound that some block reaches. `tmpl_owner`: within the 64 rows of one device no patch is named more than 16 times, a bound that some block reaches. `row_warp`: Lanczos-3 interpolation weights for a dither of 0 or plus or minus 512 / 2 rows plus a shift within 8 pixels, and a scale change within 3 / 512; rows that fall off the cutout are zero. `col_warp`: Lanczos-3 interpolation weights for a shift within 8 pixels and a scale change within 3 / 1024; every nonzero lies within 14 of the diagonal.
All inputs are finite; a program needn't handle non-finite values.
Results may differ from a plain program's by a relative error of at most 0.015.
Values may be sent and summed in bfloat16 or wider, within the bound.
A program may use at most 192 MiB of HBM per device.

v0:
```python
import functools

import jax
import jax.numpy as jnp
from jax import lax
from jax.experimental import pallas as pl
from jax.experimental.pallas import tpu as pltpu
from jax.sharding import PartitionSpec as P

BLOCK_ROWS = 16
BLOCK_COLUMNS = 128
FLOOR = 1.0
HALO = 16
SPAN = 256
STEP = 208
GROUP = 4


def conv_kernel(
    ntaps, cutout_rows, coef_ref, weight_ref, top_ref, image_ref, bottom_ref, mask_ref,
    cols_ref, rows_ref, flux_ref, ext_ref, acc_ref,
):
    nrows, width = image_ref.shape
    half = (ntaps - 1) // 2
    nwin = -(-width // STEP)
    nbasis = cols_ref.shape[0]
    left = 128
    ext = jnp.concatenate([top_ref[...], image_ref[...], bottom_ref[...]], axis=0).astype(jnp.float32)
    high = ext.shape[0]
    ext = jnp.concatenate(
        [jnp.zeros((high, left), jnp.float32), ext, jnp.zeros((high, 3 * 128), jnp.float32)], axis=1
    )
    ext_ref[...] = jnp.zeros_like(ext_ref)
    for k in range(nwin):
        start = STEP * k - half + left
        base = start // 128 * 128
        piece = ext[:, base : base + SPAN + 128]
        shift = start - base
        if shift:
            piece = pltpu.roll(piece, SPAN + 128 - shift, 1)
        ext_ref[0:high, k * SPAN : (k + 1) * SPAN] = piece[:, :SPAN].astype(jnp.bfloat16)
    first_row = lax.axis_index("tile") * nrows
    row = (first_row + lax.broadcasted_iota(jnp.int32, (nrows, SPAN), 0)).astype(jnp.float32)
    yn = (2.0 * row + 1.0) / cutout_rows - 1.0
    yy = yn * yn
    lane = lax.broadcasted_iota(jnp.int32, (1, SPAN), 1).astype(jnp.float32)
    acc_ref[...] = jnp.zeros_like(acc_ref)

    def one(b):
        taps = jnp.broadcast_to(cols_ref[pl.ds(b, 1), :], (nrows, SPAN))
        vtab = pltpu.roll(taps, 0, 1, stride=1, stride_axis=0).astype(jnp.bfloat16)
        taps = jnp.broadcast_to(rows_ref[pl.ds(b, 1), :], (SPAN, SPAN))
        htab = pltpu.roll(taps, 0, 1, stride=1, stride_axis=0).astype(jnp.bfloat16)
        vert = jnp.dot(vtab, ext_ref[...], preferred_element_type=jnp.float32).astype(jnp.bfloat16)
        c = [coef_ref[b, p] for p in range(6)]
        yyc = yy * c[3]
        stacked = jnp.concatenate([vert[:, k * SPAN : (k + 1) * SPAN] for k in range(nwin)], axis=0)
        horiz = jnp.dot(stacked, htab, preferred_element_type=jnp.float32)
        out = []
        for k in range(nwin):
            xn = (2.0 * (lane + float(STEP * k)) + 1.0) / width - 1.0
            even = c[0] + xn * (c[2] + xn * c[5])
            slope = c[1] + xn * c[4]
            out.append((yyc + even + yn * slope) * horiz[k * nrows : (k + 1) * nrows])
        return out

    def body(g, carry):
        total = one(g * GROUP)
        for u in range(1, GROUP):
            total = [a + b for a, b in zip(total, one(g * GROUP + u))]
        for k in range(nwin):
            acc_ref[k] += total[k]
        return carry

    lax.fori_loop(0, nbasis // GROUP, body, 0)
    conv = jnp.concatenate([acc_ref[k][:, :STEP] for k in range(nwin)], axis=1)[:, :width]
    bad = jnp.bitwise_and(mask_ref[...], 3) == 3
    plane = jnp.where(bad, 0.0, weight_ref[0]).astype(jnp.bfloat16).astype(jnp.float32)
    flux_ref[...] = (plane * conv).astype(jnp.bfloat16)


def convolve(image, top, bottom, mask, weight, coef, basis_cols, basis_rows, cutout_rows):
    nrows, width = image.shape
    nb, ntaps = basis_cols.shape
    half = (ntaps - 1) // 2
    padb = -nb % GROUP
    nwin = -(-width // STEP)
    cols = jnp.pad(
        basis_cols.astype(jnp.float32),
        ((0, padb), (HALO - half, SPAN - ntaps - (HALO - half))),
    )
    rows = basis_rows.astype(jnp.float32)
    rows = jnp.concatenate(
        [rows[:, :1], jnp.zeros((nb, SPAN - ntaps), jnp.float32), rows[:, :0:-1]], axis=1
    )
    rows = jnp.pad(rows, ((0, padb), (0, 0)))
    coef = jnp.pad(coef, ((0, padb), (0, 0)))
    smem = pl.BlockSpec(memory_space=pltpu.SMEM)
    vmem = pl.BlockSpec(memory_space=pltpu.VMEM)
    return pl.pallas_call(
        functools.partial(conv_kernel, ntaps, cutout_rows),
        out_shape=jax.ShapeDtypeStruct((nrows, width), jnp.bfloat16),
        in_specs=[smem, smem] + [vmem] * 6,
        out_specs=vmem,
        scratch_shapes=[
            pltpu.VMEM((SPAN, nwin * SPAN), jnp.bfloat16),
            pltpu.VMEM((nwin, nrows, SPAN), jnp.float32),
        ],
        compiler_params=pltpu.CompilerParams(vmem_limit_bytes=40 << 20),
        cost_estimate=pl.CostEstimate(flops=10 * 10**9, bytes_accessed=2 << 20, transcendentals=0),
        name="conv_flux",
    )(coef, weight, top, image, bottom, mask, cols, rows)


def slot_of(owners, count, capacity):
    hits = (owners[..., :, None] == jnp.arange(count)).astype(jnp.int32)
    rank = jnp.sum((jnp.cumsum(hits, axis=-2) - 1) * hits, axis=-1)
    return owners * capacity + rank


def to_blocks(plane):
    nrows, width = plane.shape
    return (
        plane.reshape(nrows // BLOCK_ROWS, BLOCK_ROWS, width // BLOCK_COLUMNS, BLOCK_COLUMNS)
        .transpose(0, 2, 1, 3)
        .reshape(-1, BLOCK_ROWS * BLOCK_COLUMNS)
    )


def from_blocks(blocks, nrows, width):
    return (
        blocks.reshape(nrows // BLOCK_ROWS, width // BLOCK_COLUMNS, BLOCK_ROWS, BLOCK_COLUMNS)
        .transpose(0, 2, 1, 3)
        .reshape(nrows, width)
    )


def per_device(
    visit_image, mask_bits, visit_weight, basis_cols, basis_rows, kernel_coef, row_warp,
    col_warp, dest_owner, dest_block, new_science, tmpl_owner, tmpl_block,
):
    nrows, width = visit_image.shape
    ntile = lax.axis_size("tile")
    nccd = lax.axis_size("ccd")
    me = lax.axis_index("ccd")
    nblocks = nrows // BLOCK_ROWS * (width // BLOCK_COLUMNS)
    capacity = 2 * nblocks // nccd
    nslots = nccd * capacity
    down = [(i, i + 1) for i in range(ntile - 1)]
    up = [(i + 1, i) for i in range(ntile - 1)]
    top = lax.ppermute(visit_image[-HALO:], "tile", down)
    bottom = lax.ppermute(visit_image[:HALO], "tile", up)
    bad = jnp.bitwise_and(mask_bits, 3) == 3
    weight_plane = jnp.where(bad, 0.0, visit_weight[0]).astype(jnp.bfloat16)
    weights = lax.all_gather(weight_plane, "tile", axis=0, tiled=True)
    tables = lax.all_gather(
        jnp.stack([dest_owner[:, 0], dest_block, tmpl_owner[:, 0], tmpl_block]), "ccd", axis=0
    )
    flux = convolve(
        visit_image, top, bottom, mask_bits, visit_weight, kernel_coef[0], basis_cols, basis_rows,
        nrows * ntile,
    )
    fluxes = lax.all_gather(flux, "tile", axis=0, tiled=True)

    def warp(plane):
        rowed = jnp.dot(row_warp, plane, preferred_element_type=jnp.float32).astype(jnp.bfloat16)
        return jnp.dot(rowed, col_warp[0], preferred_element_type=jnp.float32).astype(jnp.bfloat16)

    slots = slot_of(dest_owner[:, 0], nccd, capacity)
    select = (slots[None, :] == jnp.arange(nslots)[:, None]).astype(jnp.bfloat16)
    tslots = slot_of(tmpl_owner[:, 0], nccd, capacity)
    tselect = (tslots[:, None] == jnp.arange(nslots)[None, :]).astype(jnp.bfloat16)

    def arriving(owners, blocks):
        rank = slot_of(owners, nccd, capacity) - owners * capacity
        mine = owners == me
        hit = (rank[:, None, :] == jnp.arange(capacity)[None, :, None]) & mine[:, None, :]
        return jnp.max(jnp.where(hit, blocks[:, None, :], -1), axis=-1).reshape(-1)

    landing = arriving(tables[:, 0], tables[:, 1])
    wanted = arriving(tables[:, 2], tables[:, 3])
    place = (landing[None, :] == jnp.arange(nblocks)[:, None]).astype(jnp.bfloat16)
    serve = (wanted[:, None] == jnp.arange(nblocks)[None, :]).astype(jnp.bfloat16)

    def swap(x):
        x = x.reshape(nccd, capacity, -1)
        y = lax.all_to_all(x, "ccd", split_axis=0, concat_axis=0, tiled=True)
        return y.reshape(nslots, -1)

    def send(plane):
        out = jnp.dot(select, to_blocks(warp(plane)), preferred_element_type=jnp.float32)
        return swap(out.astype(jnp.bfloat16))

    den = jnp.dot(place, send(weights), preferred_element_type=jnp.float32)
    num = jnp.dot(place, send(fluxes), preferred_element_type=jnp.float32)
    coadd_blocks = num / jnp.maximum(den, FLOOR)
    reply = jnp.dot(serve, coadd_blocks.astype(jnp.bfloat16), preferred_element_type=jnp.float32)
    back = swap(reply.astype(jnp.bfloat16))
    template = jnp.dot(tselect, back, preferred_element_type=jnp.float32)
    return (
        from_blocks(coadd_blocks, nrows, width),
        new_science - from_blocks(template, nrows, width),
    )


def solution(mesh):
    both = P(("ccd", "tile"), None)
    flat = P(("ccd", "tile"))
    three = P("ccd", None, None)
    return jax.shard_map(
        per_device,
        mesh=mesh,
        in_specs=(
            both, both, P("ccd"), P(), P(), three, both, three, both, flat, both, both, flat,
        ),
        out_specs=(both, both),
        check_vma=False,
    )
```

profile of v0, /device:TPU:0, one launch (start us, length us, event | category | flops | bytes accessed | tf_op | source)
XLA Modules:
  0.0 124.0 jit_solution(10709794885001588751)
XLA Ops:
  7.2 0.0 copy-start
  7.2 0.0 all-gather.5.cloned.1.call-start
  7.2 0.9 fusion.39
  8.1 1.3 %collective-permute-start.1 = (bf16[16,1024]{1,0:T(8,128)(2,1)S(1)}, bf16[16,1024]{1,0:T(8,128)(2,1)S(1)}, u32[]{:S(2)}, u32[]{:S(2)}) collective-permute-start(bf16[16,1024]{1,0:T(8,128)(2,1)S(1)} %get-tuple-element.2), channel_id=1, source_target_pairs={{1,0},{2,1},{3,2},{5,4},{6,5},{7,6},{9,8},{10,9},{11,10},{13,12},{... | collective-permute-start | bytes 98312 | tf_op jit(solution)/shard_map/ppermute | solution.py:152
  9.4 3.0 %collective-permute-start = (bf16[16,1024]{1,0:T(8,128)(2,1)S(1)}, bf16[16,1024]{1,0:T(8,128)(2,1)S(1)}, u32[]{:S(2)}, u32[]{:S(2)}) collective-permute-start(bf16[16,1024]{1,0:T(8,128)(2,1)S(1)} %get-tuple-element.3), channel_id=1, source_target_pairs={{0,1},{1,2},{2,3},{4,5},{5,6},{6,7},{8,9},{9,10},{10,11},{12,13},{... | collective-permute-start | bytes 98312 | tf_op jit(solution)/shard_map/ppermute | solution.py:151
  12.5 0.7 slice.34
  13.2 0.7 slice.35
  13.9 0.8 copy.41
  14.6 0.1 copy.57
  14.7 0.1 rev.3
  14.8 0.1 copy.58
  14.9 0.1 pad.19.clone
  15.0 0.1 pad_maximum_fusion
  15.1 0.1 pad_convert_fusion.cols_ref
  15.8 0.8 copy.40
  16.6 0.0 copy-start.8
  16.6 0.0 collective-permute-done.1.bottom_ref
  16.6 0.0 collective-permute-done.top_ref
  16.7 0.0 copy-start.1
  16.7 1.0 copy-done.1
  17.7 0.9 copy-done.3
  18.7 10.6 %conv_flux.1 = bf16[128,1024]{1,0:T(8,128)(2,1)} custom-call(f32[32,6]{1,0:T(8,128)S(1)} %pad.14.coef_ref, f32[1]{0:T(128)} %copy.59.weight_ref, bf16[16,1024]{1,0:T(8,128)(2,1)S(1)} %collective-permute-done.top_ref, bf16[128,1024]{1,0:T(8,128)(2,1)S(1)} %copy-done.3, bf16[16,1024]{1,0:T(8,128)(2,1)S(1)} %collective-permute-done.1.bottom_ref, ...), custom_call_target="tpu_custom_call" | custom-call | flops 10000000000 | bytes 2097152 | tf_op jit(solution)/shard_map/conv_flux/pallas_call | solution.py:100
  29.3 0.0 all-gather.5.cloned.1.call-update
  29.3 0.0 all-gather.7.cloned.1.call-start
  29.4 0.0 copy-done.2
  29.4 0.8 select_convert_fusion
  30.1 0.0 all-gather.7.cloned.1.call-update
  30.2 0.1 fusion.30
  30.2 0.1 reduce_window_sum.35
  30.4 27.8 %all-gather.1 = s32[8,4,64]{2,1,0:T(4,128)S(1)} all-gather(s32[1,4,64]{2,1,0:T(4,128)S(1)} %add_bitcast_fusion), channel_id=2, replica_groups=mesh['ccd'=8,'tile'=4] {'ccd'}, dimensions={0}, use_global_device_ids=true | all-gather | bytes 9216 | tf_op jit(solution)/shard_map/all_gather | solution.py:156
  58.2 0.2 select_reduce_fusion.3
  58.4 0.0 all-gather.5.cloned.1.call-done
  58.4 2.4 %fusion.14 = bf16[16,8,8,128]{3,1,2,0:T(8,128)(2,1)S(1)} fusion(bf16[1,1024,1024]{2,1,0:T(8,128)(2,1)S(1)} %copy-done, bf16[512,1024]{1,0:T(8,128)(2,1)} %all-gather.5.cloned.1.call-done, bf16[128,512]{1,0:T(8,128)(2,1)S(1)} %copy-done.4), kind=kOutput, calls=%fused_computation.14 | convolution fusion | flops 402915328 | bytes 3538944 | tf_op jit(solution)/shard_map/dot_general | solution.py:167
  60.9 1.1 convolution_convert_fusion.2
  62.0 4.0 %all-to-all-start = ((bf16[8,16,2048]{2,1,0:T(8,128)(2,1)}), bf16[8,16,2048]{2,1,0:T(8,128)(2,1)S(1)}, u32[]{:S(2)}, u32[]{:S(2)}) async-start(bf16[8,16,2048]{2,1,0:T(8,128)(2,1)} %bitcast.13), calls=%async_computation | async-start | bytes 1048576 | tf_op jit(solution)/shard_map/all_to_all | solution.py:187
  66.0 0.1 copy.38
  66.1 1.3 %fusion.41 = s32[8,64]{0,1:T(8,128)S(1)} fusion(s32[8,64]{0,1:T(8,128)S(1)} %copy.38), kind=kOutput, calls=%fused_computation.67 | output fusion | flops 282112 | bytes 4096 | tf_op jit(solution)/shard_map/jit(cumsum)/reduce_window_sum | solution.py:117
  67.4 0.1 copy.39
  67.5 0.3 all-gather.7.cloned.1.call-done
  67.8 2.4 %fusion.11 = bf16[16,8,8,128]{3,1,2,0:T(8,128)(2,1)S(1)} fusion(bf16[1,1024,1024]{2,1,0:T(8,128)(2,1)S(1)} %copy-done, bf16[512,1024]{1,0:T(8,128)(2,1)} %all-gather.7.cloned.1.call-done, bf16[128,512]{1,0:T(8,128)(2,1)S(1)} %copy-done.4), kind=kOutput, calls=%fused_computation.13 | convolution fusion | flops 402915328 | bytes 3538944 | tf_op jit(solution)/shard_map/dot_general | solution.py:167
  70.3 1.1 convolution_convert_fusion.1
  71.3 6.4 %all-to-all-done = bf16[8,16,2048]{2,1,0:T(8,128)(2,1)S(1)} async-done(((bf16[8,16,2048]{2,1,0:T(8,128)(2,1)}), bf16[8,16,2048]{2,1,0:T(8,128)(2,1)S(1)}, u32[]{:S(2)}, u32[]{:S(2)}) %all-to-all-start) | async-done | bytes 524320 | tf_op jit(solution)/shard_map/all_to_all | solution.py:187
  77.8 3.7 %all-to-all-start.1 = ((bf16[8,16,2048]{2,1,0:T(8,128)(2,1)}), bf16[8,16,2048]{2,1,0:T(8,128)(2,1)S(1)}, u32[]{:S(2)}, u32[]{:S(2)}) async-start(bf16[8,16,2048]{2,1,0:T(8,128)(2,1)} %bitcast.18), calls=%async_computation.1 | async-start | bytes 1048576 | tf_op jit(solution)/shard_map/all_to_all | solution.py:187
  81.5 0.2 select_reduce_fusion.1
  81.7 0.1 eq.182
  81.8 0.1 copy.44
  81.8 1.3 %fusion.42 = s32[8,64]{0,1:T(8,128)S(1)} fusion(s32[8,64]{0,1:T(8,128)S(1)} %copy.44), kind=kOutput, calls=%fused_computation.68 | output fusion | flops 282112 | bytes 4096 | tf_op jit(solution)/shard_map/jit(cumsum)/reduce_window_sum | solution.py:117
  83.2 0.1 copy.45
  83.2 0.2 select_reduce_fusion
  83.4 0.1 eq.210
  83.5 1.0 fusion.31
  84.5 10.1 %all-to-all-done.1 = bf16[8,16,2048]{2,1,0:T(8,128)(2,1)S(1)} async-done(((bf16[8,16,2048]{2,1,0:T(8,128)(2,1)}), bf16[8,16,2048]{2,1,0:T(8,128)(2,1)S(1)}, u32[]{:S(2)}, u32[]{:S(2)}) %all-to-all-start.1) | async-done | bytes 524320 | tf_op jit(solution)/shard_map/all_to_all | solution.py:187
  94.7 1.3 %fusion = f32[64,2048]{1,0:T(8,128)S(1)} fusion(f32[64,2048]{1,0:T(8,128)} %fusion.31, bf16[128,2048]{1,0:T(8,128)(2,1)S(1)} %bitcast.112, s32[128]{0:T(128)S(1)} %eq.182), kind=kOutput, calls=%fused_computation.4 | convolution fusion | flops 33824768 | bytes 1573376 | tf_op jit(solution)/shard_map/dot_general | solution.py:194
  96.0 1.1 convolution_convert_fusion
  97.1 3.7 %all-to-all-start.2 = ((bf16[8,16,2048]{2,1,0:T(8,128)(2,1)}), bf16[8,16,2048]{2,1,0:T(8,128)(2,1)S(1)}, u32[]{:S(2)}, u32[]{:S(2)}) async-start(bf16[8,16,2048]{2,1,0:T(8,128)(2,1)} %bitcast.108), calls=%async_computation.2 | async-start | bytes 1048576 | tf_op jit(solution)/shard_map/all_to_all | solution.py:187
  100.8 0.1 fusion.27
  100.9 0.1 reduce_window_sum.36
  101.0 0.2 select_reduce_fusion.2
  101.2 0.1 eq.197
  101.2 0.9 copy.56
  102.1 12.4 %all-to-all-done.2 = bf16[8,16,2048]{2,1,0:T(8,128)(2,1)S(1)} async-done(((bf16[8,16,2048]{2,1,0:T(8,128)(2,1)}), bf16[8,16,2048]{2,1,0:T(8,128)(2,1)S(1)}, u32[]{:S(2)}, u32[]{:S(2)}) %all-to-all-start.2) | async-done | bytes 524320 | tf_op jit(solution)/shard_map/all_to_all | solution.py:187
  114.6 0.3 copy.46
  114.9 0.3 fusion.33
  115.2 2.0 %bitcast_subtract_fusion = f32[128,1024]{1,0:T(8,128)} fusion(f32[128,1024]{1,0:T(8,128)} %param.23, f32[16,8,8,128]{3,2,1,0:T(8,128)S(1)} %bitcast.104), kind=kLoop, calls=%fused_computation.19 | loop fusion | flops 131072 | bytes 1572864 | tf_op jit(solution)/shard_map/sub | solution.py:202
  (22 shorter events, 0.2 us)
Async XLA Ops:
  7.2 51.2 %copy-start = (bf16[1,1024,1024]{2,1,0:T(8,128)(2,1)S(1)}, bf16[1,1024,1024]{2,1,0:T(8,128)(2,1)}, u32[]{:S(2)}) copy-start(bf16[1,1024,1024]{2,1,0:T(8,128)(2,1)} %param.20) | copy-start | bytes 6291460
  7.2 51.2 %all-gather.5.cloned.1.call-start = ((), (), s32[]{:S(2)}) async-start(), calls=%async_computation.3 | async-start | bytes 1310720 | tf_op jit(solution)/shard_map/all_gather | solution.py:163
  8.1 8.5 %collective-permute-start.1 = (bf16[16,1024]{1,0:T(8,128)(2,1)S(1)}, bf16[16,1024]{1,0:T(8,128)(2,1)S(1)}, u32[]{:S(2)}, u32[]{:S(2)}) collective-permute-start(bf16[16,1024]{1,0:T(8,128)(2,1)S(1)} %get-tuple-element.2), channel_id=1, source_target_pairs={{1,0},{2,1},{3,2},{5,4},{6,5},{7,6},{9,8},{10,9},{11,10},{13,12},{... | collective-permute-start | bytes 98312 | tf_op jit(solution)/shard_map/ppermute | solution.py:152
  9.4 7.2 %collective-permute-start = (bf16[16,1024]{1,0:T(8,128)(2,1)S(1)}, bf16[16,1024]{1,0:T(8,128)(2,1)S(1)}, u32[]{:S(2)}, u32[]{:S(2)}) collective-permute-start(bf16[16,1024]{1,0:T(8,128)(2,1)S(1)} %get-tuple-element.3), channel_id=1, source_target_pairs={{0,1},{1,2},{2,3},{4,5},{5,6},{6,7},{8,9},{9,10},{10,11},{12,13},{... | collective-permute-start | bytes 98312 | tf_op jit(solution)/shard_map/ppermute | solution.py:151
  16.6 13.6 %copy-start.5 = (s32[64,1]{0,1:T(1,128)S(1)}, s32[64,1]{0,1:T(1,128)}, u32[]{:S(2)}) copy-start(s32[64,1]{0,1:T(1,128)} %param.21) | copy-start | bytes 772
  16.6 13.7 %copy-start.6 = (s32[64,1]{0,1:T(1,128)S(1)}, s32[64,1]{0,1:T(1,128)}, u32[]{:S(2)}) copy-start(s32[64,1]{0,1:T(1,128)} %param.24) | copy-start | bytes 772
  16.6 13.7 %copy-start.7 = (s32[64]{0:T(128)S(1)}, s32[64]{0:T(128)}, u32[]{:S(2)}) copy-start(s32[64]{0:T(128)} %param.25) | copy-start | bytes 772
  16.6 13.7 %copy-start.8 = (s32[64]{0:T(128)S(1)}, s32[64]{0:T(128)}, u32[]{:S(2)}) copy-start(s32[64]{0:T(128)} %param.22) | copy-start | bytes 772
  16.7 1.0 copy-start.1
  17.7 0.9 copy-start.3
  18.7 10.7 %copy-start.2 = (s32[128,1024]{1,0:T(8,128)S(1)}, s32[128,1024]{1,0:T(8,128)}, u32[]{:S(2)}) copy-start(s32[128,1024]{1,0:T(8,128)} %mask_ref.1) | copy-start | bytes 1572868
  18.7 39.7 %copy-start.4 = (bf16[128,512]{1,0:T(8,128)(2,1)S(1)}, bf16[128,512]{1,0:T(8,128)(2,1)}, u32[]{:S(2)}) copy-start(bf16[128,512]{1,0:T(8,128)(2,1)} %param.19) | copy-start | bytes 393220
  29.3 38.5 %all-gather.7.cloned.1.call-start = ((), (), s32[]{:S(2)}) async-start(), calls=%async_computation.4 | async-start | bytes 1310720 | tf_op jit(solution)/shard_map/all_gather | solution.py:155
  62.0 15.8 %all-to-all-start = ((bf16[8,16,2048]{2,1,0:T(8,128)(2,1)}), bf16[8,16,2048]{2,1,0:T(8,128)(2,1)S(1)}, u32[]{:S(2)}, u32[]{:S(2)}) async-start(bf16[8,16,2048]{2,1,0:T(8,128)(2,1)} %bitcast.13), calls=%async_computation | async-start | bytes 1048576 | tf_op jit(solution)/shard_map/all_to_all | solution.py:187
  77.8 16.9 %all-to-all-start.1 = ((bf16[8,16,2048]{2,1,0:T(8,128)(2,1)}), bf16[8,16,2048]{2,1,0:T(8,128)(2,1)S(1)}, u32[]{:S(2)}, u32[]{:S(2)}) async-start(bf16[8,16,2048]{2,1,0:T(8,128)(2,1)} %bitcast.18), calls=%async_computation.1 | async-start | bytes 1048576 | tf_op jit(solution)/shard_map/all_to_all | solution.py:187
  97.1 17.5 %all-to-all-start.2 = ((bf16[8,16,2048]{2,1,0:T(8,128)(2,1)}), bf16[8,16,2048]{2,1,0:T(8,128)(2,1)S(1)}, u32[]{:S(2)}, u32[]{:S(2)}) async-start(bf16[8,16,2048]{2,1,0:T(8,128)(2,1)} %bitcast.108), calls=%async_computation.2 | async-start | bytes 1048576 | tf_op jit(solution)/shard_map/all_to_all | solution.py:187
Sparse Core Ops, SparseCore 0:
  29.4 19.4 all-gather.4
  51.0 16.7 all-gather.6
where the time goes:
time: 125 us; the launch traced here: 124 us
  waiting for transfers between devices  29.4 us (24%)
  blocking collectives  27.8 us (22%)
  starting transfers between devices  15.8 us (13%)
  between operations  14.9 us (12%)
  matrix products  10.8 us (9%)
  Pallas kernels  10.6 us (8%)
  local copies, waits for them, and re-layouts  8.05 us (6%)
  other arithmetic  6.67 us (5%)
    all_to_all x3, waiting for transfers between devices, swap(): y = lax.all_to_all(x, 'ccd', split_axis=0, concat_axis=0, tiled=True)  29 us
    all_gather x1, blocking collectives, per_device(): lax.all_gather(jnp.stack([dest_owner[:, 0], dest_block, tmpl_owner[:, 0],...  27.8 us
    all_to_all x3, starting transfers between devices, swap(): y = lax.all_to_all(x, 'ccd', split_axis=0, concat_axis=0, tiled=True)  11.4 us
    pallas_call x1, Pallas kernels, convolve(): pl.pallas_call(functools.partial(conv_kernel, ntaps, cutout_rows), out_sh...  10.6 us
    dot_general x2, matrix products, warp(): jnp.dot(rowed, col_warp[0], preferred_element_type=jnp.float32)  4.87 us
    unnamed x25, local copies, waits for them, and re-layouts  4.77 us
    ppermute x1, starting transfers between devices, per_device(): top = lax.ppermute(visit_image[-HALO:], 'tile', down)  3.03 us
    another operation x4, other arithmetic, slot_of(): rank = jnp.sum((jnp.cumsum(hits, axis=-2) - 1) * hits, axis=-1)  2.81 us
  transfers between devices with their start and end apart: 7, of which 4 were waited for; matrix products, arithmetic and copies ran while one was open for 14% of the time, Pallas kernels for 0%

commit v1 on v0

--- a/solution.py
+++ b/solution.py
@@ -118,21 +118,127 @@
     return owners * capacity + rank
 
 
-def to_blocks(plane):
-    nrows, width = plane.shape
-    return (
-        plane.reshape(nrows // BLOCK_ROWS, BLOCK_ROWS, width // BLOCK_COLUMNS, BLOCK_COLUMNS)
-        .transpose(0, 2, 1, 3)
-        .reshape(-1, BLOCK_ROWS * BLOCK_COLUMNS)
-    )
-
-
 def from_blocks(blocks, nrows, width):
     return (
         blocks.reshape(nrows // BLOCK_ROWS, width // BLOCK_COLUMNS, BLOCK_ROWS, BLOCK_COLUMNS)
         .transpose(0, 2, 1, 3)
         .reshape(nrows, width)
     )
+
+
+MESH = pl.DeviceIdType.MESH
+
+
+def exchange_kernel(
+    nccd, source_ref, flux_ref, own_ref, across_ref, row_ref, col_ref, wout_ref, fout_ref,
+    planes, blocks, outgoing, arriving, hop_send, hop_recv, send_sem, recv_sem,
+):
+    nrows, width = flux_ref.shape
+    across_columns = width // BLOCK_COLUMNS
+    ccd, tile = lax.axis_index("ccd"), lax.axis_index("tile")
+    mate = tile + 1 - 2 * lax.rem(tile, 2)
+    opposite = lax.rem(tile + 2, 4)
+    far = lax.rem(mate + 2, 4)
+    barrier = pltpu.get_barrier_semaphore()
+    for near in (mate, opposite):
+        pl.semaphore_signal(barrier, inc=1, device_id=(ccd, near), device_id_type=MESH)
+    for d in range(1, nccd):
+        pl.semaphore_signal(
+            barrier, inc=1, device_id=(lax.rem(ccd + d, nccd), tile), device_id_type=MESH
+        )
+    pl.semaphore_wait(barrier, nccd + 1)
+
+    def hop(index, source, slot, target):
+        copy = pltpu.make_async_remote_copy(
+            src_ref=source, dst_ref=planes.at[slot], send_sem=hop_send.at[index],
+            recv_sem=hop_recv.at[index], device_id=(ccd, target), device_id_type=MESH,
+        )
+        copy.start()
+        return copy
+
+    flux_far = hop(0, flux_ref, 1, opposite)
+    own_mate = hop(1, own_ref, 2, mate)
+    across_mate = hop(2, across_ref, 3, mate)
+    flux_mate = hop(3, flux_ref, 0, mate)
+
+    def part(position, plane):
+        columns = pl.ds(pl.multiple_of(position * nrows, 128), nrows)
+        return jnp.dot(row_ref[:, columns], plane, preferred_element_type=jnp.float32)
+
+    def push(k, own, mates, opposites, fars):
+        rowed = part(tile, own) + part(mate, mates) + part(opposite, opposites) + part(far, fars)
+        warped = jnp.dot(
+            rowed.astype(jnp.bfloat16), col_ref[...], preferred_element_type=jnp.float32
+        ).astype(jnp.bfloat16)
+        for i in range(nrows // BLOCK_ROWS):
+            for j in range(across_columns):
+                blocks[k, i * across_columns + j] = warped[
+                    i * BLOCK_ROWS : (i + 1) * BLOCK_ROWS,
+                    j * BLOCK_COLUMNS : (j + 1) * BLOCK_COLUMNS,
+                ]
+        capacity = outgoing.shape[2]
+        copies = []
+        for step in range(nccd):
+            d = (step + 1) % nccd
+            target = outgoing if d else arriving
+
+            def fill(c, carry):
+                target[k, d, c] = blocks[k, source_ref[d * capacity + c]]
+                return carry
+
+            lax.fori_loop(0, capacity, fill, 0, unroll=True)
+            if d:
+                copy = pltpu.make_async_remote_copy(
+                    src_ref=outgoing.at[k, d], dst_ref=arriving.at[k, d],
+                    send_sem=send_sem.at[k, d], recv_sem=recv_sem.at[k, d],
+                    device_id=(lax.rem(ccd + d, nccd), tile), device_id_type=MESH,
+                )
+                copy.start()
+                copies.append(copy)
+        return copies
+
+    own_mate.wait()
+    across_mate.wait()
+    copies = push(0, own_ref[...], planes[2], across_ref[...], planes[3])
+    flux_far.wait()
+    flux_last = hop(4, planes.at[1], 4, mate)
+    flux_mate.wait()
+    flux_last.wait()
+    copies += push(1, flux_ref[...], planes[0], planes[1], planes[4])
+    for copy in copies[: nccd - 1]:
+        copy.wait()
+    wout_ref[...] = arriving[0]
+    for copy in copies[nccd - 1 :]:
+        copy.wait()
+    fout_ref[...] = arriving[1]
+
+
+def exchange(source, flux, own, across, row_warp, col_warp, nccd, capacity):
+    nrows, width = flux.shape
+    nblocks = nrows // BLOCK_ROWS * (width // BLOCK_COLUMNS)
+    shape = (nccd, capacity, BLOCK_ROWS, BLOCK_COLUMNS)
+    vmem = pl.BlockSpec(memory_space=pltpu.VMEM)
+    return pl.pallas_call(
+        functools.partial(exchange_kernel, nccd),
+        out_shape=[jax.ShapeDtypeStruct(shape, jnp.bfloat16)] * 2,
+        in_specs=[pl.BlockSpec(memory_space=pltpu.SMEM)] + [vmem] * 5,
+        out_specs=[vmem, vmem],
+        scratch_shapes=[
+            pltpu.VMEM((5, nrows, width), jnp.bfloat16),
+            pltpu.VMEM((2, nblocks, BLOCK_ROWS, BLOCK_COLUMNS), jnp.bfloat16),
+            pltpu.VMEM((2,) + shape, jnp.bfloat16),
+            pltpu.VMEM((2,) + shape, jnp.bfloat16),
+            pltpu.SemaphoreType.DMA((5,)),
+            pltpu.SemaphoreType.DMA((5,)),
+            pltpu.SemaphoreType.DMA((2, nccd)),
+            pltpu.SemaphoreType.DMA((2, nccd)),
+        ],
+        compiler_params=pltpu.CompilerParams(
+            vmem_limit_bytes=40 << 20, collective_id=0, has_side_effects=True
+        ),
+        cost_estimate=pl.CostEstimate(flops=10**9, bytes_accessed=6 << 20, transcendentals=0),
+        name="gather_warp_exchange",
+    )(source, flux, own, across, row_warp, col_warp)
 
 
 def per_device(
@@ -152,7 +258,7 @@
     bottom = lax.ppermute(visit_image[:HALO], "tile", up)
     bad = jnp.bitwise_and(mask_bits, 3) == 3
     weight_plane = jnp.where(bad, 0.0, visit_weight[0]).astype(jnp.bfloat16)
-    weights = lax.all_gather(weight_plane, "tile", axis=0, tiled=True)
+    across = lax.ppermute(weight_plane, "tile", [(i, (i + 2) % ntile) for i in range(ntile)])
     tables = lax.all_gather(
         jnp.stack([dest_owner[:, 0], dest_block, tmpl_owner[:, 0], tmpl_block]), "ccd", axis=0
     )
@@ -160,14 +266,11 @@
         visit_image, top, bottom, mask_bits, visit_weight, kernel_coef[0], basis_cols, basis_rows,
         nrows * ntile,
     )
-    fluxes = lax.all_gather(flux, "tile", axis=0, tiled=True)
-
-    def warp(plane):
-        rowed = jnp.dot(row_warp, plane, preferred_element_type=jnp.float32).astype(jnp.bfloat16)
-        return jnp.dot(rowed, col_warp[0], preferred_element_type=jnp.float32).astype(jnp.bfloat16)
-
     slots = slot_of(dest_owner[:, 0], nccd, capacity)
-    select = (slots[None, :] == jnp.arange(nslots)[:, None]).astype(jnp.bfloat16)
+    order = jnp.arange(nccd)
+    target_slots = ((me + order) % nccd)[:, None] * capacity + jnp.arange(capacity)[None, :]
+    select = slots[None, :] == target_slots.reshape(-1)[:, None]
+    source = jnp.sum(jnp.where(select, jnp.arange(nblocks)[None, :], 0), axis=1).astype(jnp.int32)
     tslots = slot_of(tmpl_owner[:, 0], nccd, capacity)
     tselect = (tslots[:, None] == jnp.arange(nslots)[None, :]).astype(jnp.bfloat16)
 
@@ -175,10 +278,11 @@
         rank = slot_of(owners, nccd, capacity) - owners * capacity
         mine = owners == me
         hit = (rank[:, None, :] == jnp.arange(capacity)[None, :, None]) & mine[:, None, :]
-        return jnp.max(jnp.where(hit, blocks[:, None, :], -1), axis=-1).reshape(-1)
-
-    landing = arriving(tables[:, 0], tables[:, 1])
-    wanted = arriving(tables[:, 2], tables[:, 3])
+        return jnp.max(jnp.where(hit, blocks[:, None, :], -1), axis=-1)
+
+    landing = jnp.take(arriving(tables[:, 0], tables[:, 1]), (me - order) % nccd, axis=0)
+    landing = landing.reshape(-1)
+    wanted = arriving(tables[:, 2], tables[:, 3]).reshape(-1)
     place = (landing[None, :] == jnp.arange(nblocks)[:, None]).astype(jnp.bfloat16)
     serve = (wanted[:, None] == jnp.arange(nblocks)[None, :]).astype(jnp.bfloat16)
 
@@ -187,12 +291,12 @@
         y = lax.all_to_all(x, "ccd", split_axis=0, concat_axis=0, tiled=True)
         return y.reshape(nslots, -1)
 
-    def send(plane):
-        out = jnp.dot(select, to_blocks(warp(plane)), preferred_element_type=jnp.float32)
-        return swap(out.astype(jnp.bfloat16))
-
-    den = jnp.dot(place, send(weights), preferred_element_type=jnp.float32)
-    num = jnp.dot(place, send(fluxes), preferred_element_type=jnp.float32)
+    arrived = exchange(
+        source, flux, weight_plane, across, row_warp, col_warp[0], nccd, capacity
+    )
+    den, num = (
+        jnp.dot(place, x.reshape(nslots, -1), preferred_element_type=jnp.float32) for x in arrived
+    )
     coadd_blocks = num / jnp.maximum(den, FLOOR)
     reply = jnp.dot(serve, coadd_blocks.astype(jnp.bfloat16), preferred_element_type=jnp.float32)
     back = swap(reply.astype(jnp.bfloat16))

time: 125 us -> 114 us (0.912)
  Pallas kernels: 10.6 us -> 37.1 us
  waiting for transfers between devices: 29.4 us -> 13.1 us
  between operations: 14.9 us -> 1.48 us
  matrix products: 10.8 us -> 1.95 us
  other arithmetic: 6.67 us -> 8.94 us
  blocking collectives: 27.8 us -> 26.3 us
    pallas_call x0 -> x1, Pallas kernels: none -> 27.2 us  [exchange(): pl.pallas_call(functools.partial(exchange_kernel, nccd), out_shape=[jax.S...]
    all_to_all x3 -> x1, waiting for transfers between devices: 29 us -> 13.1 us  [swap(): y = lax.all_to_all(x, 'ccd', split_axis=0, concat_axis=0, tiled=True)]
    dot_general x6 -> x2, matrix products: 9.31 us -> 0.48 us  [per_device(): jnp.dot(place, x.reshape(nslots, -1), preferred_element_type=jnp.float32)]
    ppermute x0 -> x1, starting transfers between devices: none -> 4.94 us  [per_device(): lax.ppermute(weight_plane, 'tile', [(i, (i + 2) % ntile) for i in range(n...]
    all_to_all x3 -> x1, starting transfers between devices: 11.4 us -> 7.87 us  [swap(): y = lax.all_to_all(x, 'ccd', split_axis=0, concat_axis=0, tiled=True)]
    all_gather x1, blocking collectives: 27.8 us -> 26.3 us  [per_device(): lax.all_gather(jnp.stack([dest_owner[:, 0], dest_block, tmpl_owner[:, 0],...]
    unnamed x25 -> x17, local copies, waits for them, and re-layouts: 4.77 us -> 4.67 us
  transfers between devices with their start and end apart: 7 -> 4, of which waited for: 4 -> 1; matrix products, arithmetic and copies ran while one was open for 14% -> 12% of each run, Pallas kernels for 0% -> 9%
where the time goes in v1:
time: 114 us
  Pallas kernels  37.1 us (33%)
  blocking collectives  26.3 us (23%)
  starting transfers between devices  16.4 us (14%)
  waiting for transfers between devices  13.1 us (11%)
  other arithmetic  8.94 us (8%)
  local copies, waits for them, and re-layouts  8.43 us (7%)
  matrix products  1.95 us (2%)
  between operations  1.48 us (1%)
    pallas_call x1, Pallas kernels, exchange(): pl.pallas_call(functools.partial(exchange_kernel, nccd), out_shape=[jax.S...  27.2 us
    all_gather x1, blocking collectives, per_device(): lax.all_gather(jnp.stack([dest_owner[:, 0], dest_block, tmpl_owner[:, 0],...  26.3 us
    all_to_all x1, waiting for transfers between devices, swap(): y = lax.all_to_all(x, 'ccd', split_axis=0, concat_axis=0, tiled=True)  13.1 us
    pallas_call x1, Pallas kernels, convolve(): pl.pallas_call(functools.partial(conv_kernel, ntaps, cutout_rows), out_sh...  9.91 us
    all_to_all x1, starting transfers between devices, swap(): y = lax.all_to_all(x, 'ccd', split_axis=0, concat_axis=0, tiled=True)  7.87 us
    ppermute x1, starting transfers between devices, per_device(): lax.ppermute(weight_plane, 'tile', [(i, (i + 2) % ntile) for i in range(n...  4.94 us
    unnamed x17, local copies, waits for them, and re-layouts  4.67 us
    another operation x4, other arithmetic, slot_of(): rank = jnp.sum((jnp.cumsum(hits, axis=-2) - 1) * hits, axis=-1)  2.82 us
  transfers between devices with their start and end apart: 4, of which 1 were waited for; matrix products, arithmetic and copies ran while one was open for 12% of the time, Pallas kernels for 9%

profile of v1, /device:TPU:0, one launch (start us, length us, event | category | flops | bytes accessed | tf_op | source)
XLA Modules:
  0.0 113.8 jit_solution(8465220961873117238)
XLA Ops:
  0.6 0.8 fusion.30
  1.4 2.3 %collective-permute-start = (bf16[16,1024]{1,0:T(8,128)(2,1)S(1)}, bf16[16,1024]{1,0:T(8,128)(2,1)S(1)}, u32[]{:S(2)}, u32[]{:S(2)}) collective-permute-start(bf16[16,1024]{1,0:T(8,128)(2,1)S(1)} %get-tuple-element.7), channel_id=1, source_target_pairs={{0,1},{1,2},{2,3},{4,5},{5,6},{6,7},{8,9},{9,10},{10,11},{12,13},{... | collective-permute-start | bytes 98312 | tf_op jit(solution)/shard_map/ppermute | solution.py:257
  3.8 1.3 %collective-permute-start.1 = (bf16[16,1024]{1,0:T(8,128)(2,1)S(1)}, bf16[16,1024]{1,0:T(8,128)(2,1)S(1)}, u32[]{:S(2)}, u32[]{:S(2)}) collective-permute-start(bf16[16,1024]{1,0:T(8,128)(2,1)S(1)} %get-tuple-element.6), channel_id=1, source_target_pairs={{1,0},{2,1},{3,2},{5,4},{6,5},{7,6},{9,8},{10,9},{11,10},{13,12},{... | collective-permute-start | bytes 98312 | tf_op jit(solution)/shard_map/ppermute | solution.py:258
  5.7 1.1 select_convert_fusion.own_ref
  6.8 4.9 %collective-permute-start.2 = (bf16[128,1024]{1,0:T(8,128)(2,1)S(1)}, bf16[128,1024]{1,0:T(8,128)(2,1)S(1)}, u32[]{:S(2)}, u32[]{:S(2)}) collective-permute-start(bf16[128,1024]{1,0:T(8,128)(2,1)S(1)} %select_convert_fusion.own_ref), channel_id=1, source_target_pairs={{0,2},{1,3},{2,0},{3,1},{4,6},{5,7},{6,4},{7,5},{8,10},{9,11},{10,... | collective-permute-start | bytes 786440 | tf_op jit(solution)/shard_map/ppermute | solution.py:261
  11.8 0.7 slice.37
  12.5 0.7 slice.36
  13.2 0.1 iota_add_fusion
  13.3 0.1 add.101
  13.3 0.7 fusion.17
  14.1 0.1 reduce_window_sum.35
  14.2 0.8 select_reduce_fusion.4
  15.0 0.7 multiply_add_fusion
  15.7 0.8 copy.41
  16.5 0.1 copy.65
  16.6 0.1 rev.3
  16.6 0.1 copy.66
  16.7 0.7 add_bitcast_fusion
  17.5 26.3 %all-gather.1 = s32[8,4,64]{2,1,0:T(4,128)S(1)} all-gather(s32[1,4,64]{2,1,0:T(4,128)S(1)} %add_bitcast_fusion), channel_id=2, replica_groups=mesh['ccd'=8,'tile'=4] {'ccd'}, dimensions={0}, use_global_device_ids=true | all-gather | bytes 9216 | tf_op jit(solution)/shard_map/all_gather | solution.py:262
  43.8 0.1 copy.38
  43.9 1.3 %fusion.32 = s32[8,64]{0,1:T(8,128)S(1)} fusion(s32[8,64]{0,1:T(8,128)S(1)} %copy.38), kind=kOutput, calls=%fused_computation.76 | output fusion | flops 282112 | bytes 4096 | tf_op jit(solution)/shard_map/jit(cumsum)/reduce_window_sum | solution.py:117
  45.2 0.1 copy.39
  45.3 0.1 copy.44
  45.4 1.3 %fusion.33 = s32[8,64]{0,1:T(8,128)S(1)} fusion(s32[8,64]{0,1:T(8,128)S(1)} %copy.44), kind=kOutput, calls=%fused_computation.77 | output fusion | flops 282112 | bytes 4096 | tf_op jit(solution)/shard_map/jit(cumsum)/reduce_window_sum | solution.py:117
  46.7 0.1 copy.45
  46.7 0.1 select_reduce_fusion.3.source_ref
  46.8 0.1 pad.19.clone
  46.9 0.2 select_reduce_fusion.1
  47.2 0.6 gather_fusion
  47.7 0.1 broadcast_select_fusion
  47.8 0.1 pad_maximum_fusion
  47.9 0.2 select_reduce_fusion
  48.1 0.1 pad_convert_fusion.cols_ref
  48.2 0.8 copy.40
  48.9 0.1 select_n.74
  49.0 0.1 eq.208
  49.1 0.0 collective-permute-done.top_ref
  49.1 0.0 collective-permute-done.1.bottom_ref
  49.1 0.0 copy-start
  49.1 1.0 copy-done
  50.2 0.0 copy-start.1
  50.2 0.9 copy-done.1
  51.1 0.0 copy-start.2
  51.1 9.9 %conv_flux.1.flux_ref = bf16[128,1024]{1,0:T(8,128)(2,1)S(1)} custom-call(f32[32,6]{1,0:T(8,128)S(1)} %pad.14.coef_ref, f32[1]{0:T(128)} %copy.67.weight_ref, bf16[16,1024]{1,0:T(8,128)(2,1)S(1)} %collective-permute-done.top_ref, bf16[128,1024]{1,0:T(8,128)(2,1)S(1)} %copy-done.1, bf16[16,1024]{1,0:T(8,128)(2,1)S(1)} %collective-permute-done.1.bottom_ref, ...), custom_call_target="tpu_custom_call" | custom-call | flops 10000000000 | bytes 2097152 | tf_op jit(solution)/shard_map/conv_flux/pallas_call | solution.py:100
  61.0 0.0 collective-permute-done.2.across_ref
  61.0 0.0 copy-done.2
  61.1 0.0 copy-done.3
  61.1 27.2 %gather_warp_exchange.1 = (bf16[8,16,16,128]{3,2,1,0:T(8,128)(2,1)S(1)}, bf16[8,16,16,128]{3,2,1,0:T(8,128)(2,1)S(1)}) custom-call(s32[128]{0:T(128)S(1)} %select_reduce_fusion.3.source_ref, bf16[128,1024]{1,0:T(8,128)(2,1)S(1)} %conv_flux.1.flux_ref, bf16[128,1024]{1,0:T(8,128)(2,1)S(1)} %select_convert_fusion.own_ref, ...), custom_call_target="tpu_custom_call" | custom-call | flops 1000000000 | bytes 6291456 | tf_op jit(solution)/shard_map/gather_warp_exchange/pallas_call | solution.py:221
  88.3 0.2 fusion.5
  88.5 0.0 copy-start.5
  88.5 0.2 fusion
  88.8 1.1 %convolution_convert_fusion = bf16[128,2048]{1,0:T(8,128)(2,1)} fusion(f32[64,2048]{1,0:T(8,128)S(1)} %fusion, s32[128]{0:T(128)S(1)} %eq.208), kind=kOutput, calls=%fused_computation.1 | convolution fusion | flops 33955840 | bytes 1049088 | tf_op jit(solution)/shard_map/dot_general | solution.py:301
  89.9 7.9 %all-to-all-start = ((bf16[8,16,2048]{2,1,0:T(8,128)(2,1)}), bf16[8,16,2048]{2,1,0:T(8,128)(2,1)S(1)}, u32[]{:S(2)}, u32[]{:S(2)}) async-start(bf16[8,16,2048]{2,1,0:T(8,128)(2,1)} %bitcast.23), calls=%async_computation | async-start | bytes 1048576 | tf_op jit(solution)/shard_map/all_to_all | solution.py:291
  97.8 0.0 copy-done.5
  97.8 0.1 fusion.16
  97.9 0.1 reduce_window_sum.36
  98.0 0.2 select_reduce_fusion.2
  98.2 0.1 eq.195
  98.3 0.9 copy.64
  99.2 13.1 %all-to-all-done = bf16[8,16,2048]{2,1,0:T(8,128)(2,1)S(1)} async-done(((bf16[8,16,2048]{2,1,0:T(8,128)(2,1)}), bf16[8,16,2048]{2,1,0:T(8,128)(2,1)S(1)}, u32[]{:S(2)}, u32[]{:S(2)}) %all-to-all-start) | async-done | bytes 524320 | tf_op jit(solution)/shard_map/all_to_all | solution.py:291
  112.2 0.3 copy.46
  112.5 0.3 fusion.19
  112.9 0.0 copy-done.4
  112.9 0.9 bitcast_subtract_fusion
  (12 shorter events, 0.1 us)
Async XLA Ops:
  1.4 47.7 %collective-permute-start = (bf16[16,1024]{1,0:T(8,128)(2,1)S(1)}, bf16[16,1024]{1,0:T(8,128)(2,1)S(1)}, u32[]{:S(2)}, u32[]{:S(2)}) collective-permute-start(bf16[16,1024]{1,0:T(8,128)(2,1)S(1)} %get-tuple-element.7), channel_id=1, source_target_pairs={{0,1},{1,2},{2,3},{4,5},{5,6},{6,7},{8,9},{9,10},{10,11},{12,13},{... | collective-permute-start | bytes 98312 | tf_op jit(solution)/shard_map/ppermute | solution.py:257
  3.8 45.3 %collective-permute-start.1 = (bf16[16,1024]{1,0:T(8,128)(2,1)S(1)}, bf16[16,1024]{1,0:T(8,128)(2,1)S(1)}, u32[]{:S(2)}, u32[]{:S(2)}) collective-permute-start(bf16[16,1024]{1,0:T(8,128)(2,1)S(1)} %get-tuple-element.6), channel_id=1, source_target_pairs={{1,0},{2,1},{3,2},{5,4},{6,5},{7,6},{9,8},{10,9},{11,10},{13,12},{... | collective-permute-start | bytes 98312 | tf_op jit(solution)/shard_map/ppermute | solution.py:258
  6.8 54.2 %collective-permute-start.2 = (bf16[128,1024]{1,0:T(8,128)(2,1)S(1)}, bf16[128,1024]{1,0:T(8,128)(2,1)S(1)}, u32[]{:S(2)}, u32[]{:S(2)}) collective-permute-start(bf16[128,1024]{1,0:T(8,128)(2,1)S(1)} %select_convert_fusion.own_ref), channel_id=1, source_target_pairs={{0,2},{1,3},{2,0},{3,1},{4,6},{5,7},{6,4},{7,5},{8,10},{9,11},{10,... | collective-permute-start | bytes 786440 | tf_op jit(solution)/shard_map/ppermute | solution.py:261
  49.1 1.0 copy-start
  50.2 0.9 copy-start.1
  51.1 9.9 %copy-start.2 = (bf16[1,1024,1024]{2,1,0:T(8,128)(2,1)S(1)}, bf16[1,1024,1024]{2,1,0:T(8,128)(2,1)}, u32[]{:S(2)}) copy-start(bf16[1,1024,1024]{2,1,0:T(8,128)(2,1)} %param.20) | copy-start | bytes 6291460
  51.1 9.9 %copy-start.3 = (bf16[128,512]{1,0:T(8,128)(2,1)S(1)}, bf16[128,512]{1,0:T(8,128)(2,1)}, u32[]{:S(2)}) copy-start(bf16[128,512]{1,0:T(8,128)(2,1)} %row_ref.1) | copy-start | bytes 393220
  88.5 9.3 %copy-start.5 = (s32[64,1]{0,1:T(1,128)S(1)}, s32[64,1]{0,1:T(1,128)}, u32[]{:S(2)}) copy-start(s32[64,1]{0,1:T(1,128)} %param.24) | copy-start | bytes 772
  89.9 22.9 %copy-start.4 = (f32[128,1024]{1,0:T(8,128)S(1)}, f32[128,1024]{1,0:T(8,128)}, u32[]{:S(2)}) copy-start(f32[128,1024]{1,0:T(8,128)} %param.23) | copy-start | bytes 1572868
  89.9 22.3 %all-to-all-start = ((bf16[8,16,2048]{2,1,0:T(8,128)(2,1)}), bf16[8,16,2048]{2,1,0:T(8,128)(2,1)S(1)}, u32[]{:S(2)}, u32[]{:S(2)}) async-start(bf16[8,16,2048]{2,1,0:T(8,128)(2,1)} %bitcast.23), calls=%async_computation | async-start | bytes 1048576 | tf_op jit(solution)/shard_map/all_to_all | solution.py:291
